TPU v7x, 512 devices: a whole 4x4x16 slice. The times are simulated.
512 devices in a mesh: dp: 16 (over y, x), expert: 32 (over z, core).
Axes of the slice: x: 4, y: 4, z: 16, core: 2. Of those that a mesh axis runs over, the one named last changes fastest.
Arguments:
- inputs: bfloat16 [2048, 6144], P('expert', 'dp'), may hold values from -6 to 6
- grad_out: bfloat16 [2048, 6144], P('expert', 'dp'), may hold values from -6 to 6
- expert_ids: int32 [2048, 2], P('expert'), may hold values from 0 to 3, as said below
- live_counts: int32 [32], P('expert'), may hold values from 32 to 64, as said below
- router_weight: bfloat16 [6144, 4], P('dp'), may hold values from -0.078125 to 0.078125
- up_weight: bfloat16 [6144, 32768], P('dp', 'expert'), may hold values from -0.078125 to 0.078125
- down_weight: bfloat16 [6144, 32768], P('dp', 'expert'), may hold values from -0.0625 to 0.0625
Outputs:
- grad_inputs: bfloat16 [2048, 6144], P('expert', 'dp')
- grad_up: bfloat16 [6144, 32768], P('dp', 'expert')
- grad_down: bfloat16 [6144, 32768], P('dp', 'expert')
- grad_router: float32 [6144, 4], P('dp')
Inputs may be any that keep to these rules, and one draw needn't show every extreme that they name: `expert_ids`: each row names two different experts. Among the first live_counts[g] tokens of group g, each expert is named at most 32 times; one expert is named exactly 32 times in every group. `live_counts`: some group has all its slots live.
All inputs are finite; a program needn't handle non-finite values.
Results may differ from a plain program's by a relative error of at most 0.035.
Values may be sent and summed in bfloat16 or wider, within the bound.
A program may use at most 64 MiB of HBM per device.

v0:
```python
import jax
import jax.numpy as jnp
from jax import lax
from jax.sharding import PartitionSpec as P

ROOT_HALF = 0.7071067811865476
INV_ROOT_TWO_PI = 0.3989422804014327


def gelu_value(value):
    return 0.5 * value * (1.0 + jax.scipy.special.erf(value * ROOT_HALF))


def gelu_slope(value):
    return (
        0.5 * (1.0 + jax.scipy.special.erf(value * ROOT_HALF))
        + value * jnp.exp(-0.5 * value * value) * INV_ROOT_TWO_PI
    )


def activate(before_act, back_act, gate_column):
    active = gelu_value(before_act)
    hidden = lax.optimization_barrier(active.astype(jnp.bfloat16))
    gate_sum = jnp.sum(hidden.astype(jnp.float32) * back_act, axis=1)
    inner_grad = (gate_column * back_act * gelu_slope(before_act)).astype(jnp.bfloat16)
    weighted = (gate_column * active).astype(jnp.bfloat16)
    return (gate_sum, inner_grad, weighted)


def local(inputs, grad_out, expert_ids, live_counts, router_weight, up_weight, down_weight):
    per_group = inputs.shape[0]
    share = inputs.shape[1]
    experts = router_weight.shape[1]
    groups = lax.axis_size("expert")
    column_parts = groups // experts
    capacity = 2 * per_group // experts
    partial_logits = jnp.dot(inputs, router_weight, preferred_element_type=jnp.float32)
    logits = lax.psum(partial_logits, "dp")
    labels = jnp.arange(experts, dtype=jnp.int32)
    first_hot = (expert_ids[:, 0:1] == labels[None, :]).astype(jnp.float32)
    second_hot = (expert_ids[:, 1:2] == labels[None, :]).astype(jnp.float32)
    logit_gap = jnp.sum(logits * (first_hot - second_hot), axis=1)
    pick_gates = jnp.concatenate([jax.nn.sigmoid(logit_gap), jax.nn.sigmoid(-logit_gap)]).astype(
        jnp.bfloat16
    )
    pick_ids = jnp.concatenate([expert_ids[:, 0], expert_ids[:, 1]])
    position = jnp.arange(2 * per_group, dtype=jnp.int32) % per_group
    is_live = position < live_counts[0]
    one_hot = ((pick_ids[:, None] == labels[None, :]) & is_live[:, None]).astype(jnp.int32)
    pick_rank = jnp.sum(jnp.cumsum(one_hot, axis=0) * one_hot, axis=1) - 1
    overflow = experts * capacity
    pick_slot = jnp.where(is_live, pick_ids * capacity + pick_rank, overflow)
    slot_pick = (
        jnp.full((overflow,), 2 * per_group, jnp.int32)
        .at[pick_slot]
        .set(jnp.arange(2 * per_group, dtype=jnp.int32), mode="drop")
    )
    target = jnp.arange(groups * capacity, dtype=jnp.int32)
    expert_slot = target // capacity // column_parts * capacity + target % capacity
    send_pick = jnp.take(slot_pick, expert_slot, axis=0)
    send_token = jnp.where(send_pick < 2 * per_group, send_pick % per_group, per_group)
    send_rows = jnp.take(inputs, send_token, axis=0, mode="fill", fill_value=0)
    send_grad = jnp.take(grad_out, send_token, axis=0, mode="fill", fill_value=0)
    send_gate = jnp.take(pick_gates, send_pick, axis=0, mode="fill", fill_value=0)
    rows_in, rows_grad, gate_in = (
        lax.all_to_all(send_rows, "expert", split_axis=0, concat_axis=0, tiled=True),
        lax.all_to_all(send_grad, "expert", split_axis=0, concat_axis=0, tiled=True),
        lax.all_to_all(send_gate, "expert", split_axis=0, concat_axis=0, tiled=True),
    )
    before_part = jnp.dot(rows_in, up_weight, preferred_element_type=jnp.float32)
    back_part = jnp.dot(rows_grad, down_weight, preferred_element_type=jnp.float32)
    gate_column = gate_in.astype(jnp.float32)[:, None]
    before_act, back_act = (
        lax.psum(before_part.astype(jnp.bfloat16), "dp").astype(jnp.float32),
        lax.psum(back_part.astype(jnp.bfloat16), "dp").astype(jnp.float32),
    )
    gate_part, inner_grad, weighted = activate(before_act, back_act, gate_column)
    contract_rows = (((0,), (0,)), ((), ()))
    grad_up = lax.dot_general(
        rows_in, inner_grad, contract_rows, preferred_element_type=jnp.float32
    ).astype(jnp.bfloat16)
    grad_down = lax.dot_general(
        rows_grad, weighted, contract_rows, preferred_element_type=jnp.float32
    ).astype(jnp.bfloat16)
    contract_units = (((1,), (1,)), ((), ()))
    input_part = lax.dot_general(
        inner_grad, up_weight, contract_units, preferred_element_type=jnp.float32
    ).astype(jnp.bfloat16)
    back_rows, back_gate = (
        lax.all_to_all(input_part, "expert", split_axis=0, concat_axis=0, tiled=True),
        lax.all_to_all(
            gate_part.astype(jnp.bfloat16), "expert", split_axis=0, concat_axis=0, tiled=True
        ),
    )
    summed_rows = jnp.sum(
        back_rows.astype(jnp.float32).reshape(experts, column_parts, capacity, share), axis=1
    ).reshape(overflow, share)
    summed_gate = jnp.sum(
        back_gate.astype(jnp.float32).reshape(experts, column_parts, capacity), axis=1
    ).reshape(overflow)
    part_pick = jnp.take(summed_rows, pick_slot, axis=0, mode="fill", fill_value=0)
    gate_pick = jnp.take(summed_gate, pick_slot, axis=0, mode="fill", fill_value=0)
    gate_value = pick_gates.astype(jnp.float32)
    delta = lax.optimization_barrier(
        (gate_pick * gate_value * (1.0 - gate_value)).astype(jnp.bfloat16)
    ).astype(jnp.float32)
    delta_diff = delta[:per_group] - delta[per_group:]
    logit_grad = delta_diff[:, None] * (first_hot - second_hot)
    router_side = jnp.dot(
        logit_grad, router_weight.astype(jnp.float32).T, precision=lax.Precision.HIGHEST
    )
    grad_inputs = (
        grad_out.astype(jnp.float32) + (part_pick[:per_group] + part_pick[per_group:]) + router_side
    ).astype(jnp.bfloat16)
    router_term = jnp.dot(inputs.astype(jnp.float32).T, logit_grad, precision=lax.Precision.HIGHEST)
    grad_router = lax.psum(router_term, "expert")
    return (grad_inputs, grad_up, grad_down, grad_router)


def solution(mesh):
    placed = (
        P("expert", "dp"),
        P("expert", "dp"),
        P("expert", None),
        P("expert"),
        P("dp", None),
        P("dp", "expert"),
        P("dp", "expert"),
    )
    return jax.shard_map(
        local,
        mesh=mesh,
        in_specs=placed,
        out_specs=(P("expert", "dp"), P("dp", "expert"), P("dp", "expert"), P("dp", None)),
        check_vma=False,
    )
```

profile of v0, /device:TPU:1, one launch (start us, length us, event | category | flops | bytes accessed | tf_op | source)
XLA Modules:
  0.0 425.7 jit_solution(18165804764282503032)
XLA Ops:
  7.2 0.0 copy-start
  7.2 0.0 copy-start.2
  7.2 0.8 slice_bitcast_fusion.1
  8.6 0.1 pad_add_fusion
  8.7 0.1 fusion.17
  8.8 0.2 reduce_window_sum.11
  9.0 0.2 select_reduce_fusion
  9.2 0.1 fusion.52
  9.3 1.0 scatter_custom_fusion
  10.3 6.6 %gather_fusion = s32[1024]{0:T(1024)S(1)} fusion(s32[128]{0:T(128)S(1)} %scatter_custom_fusion, s32[1024]{0:T(1024)S(1)} %broadcast_clamp_fusion.2), kind=kCustom, calls=%fused_computation.2 | custom fusion | bytes 12288 | tf_op jit(solution)/shard_map/jit(_take)/gather | solution.py:60
  16.8 0.0 copy-start.1
  16.9 0.0 copy-done.2
  16.9 3.9 gather_fusion.4
  20.8 0.0 copy-done.1
  20.8 3.9 gather_fusion.5
  24.8 1.2 broadcast_select_fusion
  25.9 61.2 %all_to_all.45 = bf16[32,32,384]{2,1,0:T(8,128)(2,1)S(1)} all-to-all(bf16[32,32,384]{2,1,0:T(8,128)(2,1)S(1)} %bitcast.49), channel_id=1, replica_groups=mesh['dp'=16,'expert'=32] {'expert'}, dimensions={0} | all-to-all | bytes 1572864 | tf_op jit(solution)/shard_map/all_to_all | solution.py:66
  87.1 0.0 copy-start.6
  87.1 4.1 all-to-all-start.1
  91.2 0.0 all-reduce.3.cloned.1.call-start
  91.2 0.0 copy-done
  91.3 2.5 convolution_convert_fusion
  93.8 0.0 copy-start.9
  93.8 42.0 %all-to-all-done.1 = bf16[32,32,384]{2,1,0:T(8,128)(2,1)S(1)} async-done(((bf16[32,32,384]{2,1,0:T(8,128)(2,1)}), bf16[32,32,384]{2,1,0:T(8,128)(2,1)S(1)}, u32[]{:S(2)}, u32[]{:S(2)}) %all-to-all-start.1) | async-done | bytes 786464 | tf_op jit(solution)/shard_map/all_to_all | solution.py:67
  135.8 4.0 convolution_convert_fusion.1
  139.8 0.0 copy-done.6
  139.8 0.0 all-reduce.3.cloned.1.call-update
  139.9 0.0 copy-done.9
  139.9 0.1 fusion.58
  140.0 34.2 %psum.28 = f32[64,4]{0,1:T(4,128)S(1)} all-reduce(f32[64,4]{0,1:T(4,128)S(1)} %fusion.58), channel_id=1, replica_groups=mesh['dp'=16,'expert'=32] {'dp'}, use_global_device_ids=true, to_apply=%region_3.4 | all-reduce | flops 256 | bytes 2048 | tf_op jit(solution)/shard_map/psum | solution.py:38
  174.3 91.7 %all-reduce.3.cloned.1.call-done = (bf16[1024,1024]{1,0:T(8,128)(2,1)}, bf16[1024,1024]{1,0:T(8,128)(2,1)}) async-done(((bf16[1024,1024]{1,0:T(8,128)(2,1)}, bf16[1024,1024]{1,0:T(8,128)(2,1)}), (bf16[1024,1024]{1,0:T(8,128)(2,1)}, bf16[1024,1024]{1,0:T(8,128)(2,1)})) %all-reduce.3.cloned.1.call-update) | async-done | bytes 4194320 | tf_op jit(solution)/shard_map/psum | solution.py:75
  265.9 0.0 copy-done.7
  265.9 3.8 fusion.9
  269.7 0.0 copy-done.5
  269.7 0.6 fusion.2
  270.3 0.7 convert_element_type.131
  271.0 13.2 %all-to-all-start.4 = ((bf16[32,32,1]{1,2,0:T(2,128)(2,1)}), bf16[32,32,1]{1,2,0:T(2,128)(2,1)S(1)}, u32[]{:S(2)}, u32[]{:S(2)}) async-start(bf16[32,32,1]{1,2,0:T(2,128)(2,1)} %convert_element_type.131), calls=%async_computation.4 | async-start | bytes 32768 | tf_op jit(solution)/shard_map/all_to_all | solution.py:91
  284.2 0.1 gather.26
  284.3 11.6 %all-to-all-done.4 = bf16[32,32,1]{1,2,0:T(2,128)(2,1)S(1)} async-done(((bf16[32,32,1]{1,2,0:T(2,128)(2,1)}), bf16[32,32,1]{1,2,0:T(2,128)(2,1)S(1)}, u32[]{:S(2)}, u32[]{:S(2)}) %all-to-all-start.4) | async-done | bytes 2080 | tf_op jit(solution)/shard_map/all_to_all | solution.py:91
  296.0 0.1 reshape.485
  296.0 1.2 gather_fusion.3
  297.3 0.1 multiply_convert_fusion.4
  297.4 6.5 %gather_fusion.1 = bf16[1024]{0:T(1024)(128)(2,1)S(1)} fusion(bf16[128]{0:T(256)(128)(2,1)S(1)} %get-tuple-element.9, s32[1024]{0:T(1024)S(1)} %broadcast_clamp_fusion.1), kind=kCustom, calls=%fused_computation.3 | custom fusion | bytes 8192 | tf_op jit(solution)/shard_map/jit(_take)/gather | solution.py:64
  303.9 0.1 gather.29
  304.0 15.4 %all_to_all.46 = bf16[32,32,1]{1,2,0:T(2,128)(2,1)S(1)} all-to-all(bf16[32,32,1]{1,2,0:T(2,128)(2,1)S(1)} %copy.11), channel_id=1, replica_groups=mesh['dp'=16,'expert'=32] {'expert'}, dimensions={0} | all-to-all | bytes 4096 | tf_op jit(solution)/shard_map/all_to_all | solution.py:68
  319.4 0.1 convert_reduce_fusion.2
  319.5 0.1 reshape.486
  319.6 0.0 copy-done.3
  319.6 4.1 fusion.1
  323.7 0.0 copy-start.4
  323.7 2.2 convolution_convert_fusion.3
  325.8 0.0 copy-done.4
  325.8 5.1 %all-to-all-start.3 = ((bf16[32,32,384]{2,1,0:T(8,128)(2,1)}), bf16[32,32,384]{2,1,0:T(8,128)(2,1)}, u32[]{:S(2)}, u32[]{:S(2)}) async-start(bf16[32,32,384]{2,1,0:T(8,128)(2,1)} %bitcast.50), calls=%async_computation.3 | async-start | bytes 1572864 | tf_op jit(solution)/shard_map/all_to_all | solution.py:90
  330.9 0.1 slice_subtract_fusion
  331.0 0.1 convolution_bitcast_fusion
  331.1 76.7 %psum.31 = f32[384,4]{0,1:T(4,128)} all-reduce(f32[384,4]{0,1:T(4,128)S(1)} %convolution_bitcast_fusion), channel_id=1, replica_groups=mesh['dp'=16,'expert'=32] {'expert'}, use_global_device_ids=true, to_apply=%region_10.12 | all-reduce | flops 1536 | bytes 12288 | tf_op jit(solution)/shard_map/psum | solution.py:116
  407.9 3.8 convolution_convert_fusion.2
  411.6 0.0 copy-done.8
  411.7 4.2 fusion.13
  415.8 0.0 all-to-all-done.3
  415.8 1.3 convert_reduce_fusion
  417.1 0.8 gather_fusion.2
  417.9 0.1 broadcast_select_fusion.2
  418.0 0.9 fusion.14
  (19 shorter events, 0.2 us)
Async XLA Ops:
  7.2 84.1 %copy-start = (bf16[384,1024]{1,0:T(8,128)(2,1)S(1)}, bf16[384,1024]{1,0:T(8,128)(2,1)}, u32[]{:S(2)}) copy-start(bf16[384,1024]{1,0:T(8,128)(2,1)} %param.14) | copy-start | bytes 2359300
  7.2 9.7 %copy-start.2 = (bf16[64,384]{1,0:T(8,128)(2,1)S(1)}, bf16[64,384]{1,0:T(8,128)(2,1)}, u32[]{:S(2)}) copy-start(bf16[64,384]{1,0:T(8,128)(2,1)} %param.10) | copy-start | bytes 147460
  16.8 4.0 copy-start.1
  87.1 52.7 %copy-start.6 = (bf16[32,32,384]{2,1,0:T(8,128)(2,1)}, bf16[32,32,384]{2,1,0:T(8,128)(2,1)S(1)}, u32[]{:S(2)}) copy-start(bf16[32,32,384]{2,1,0:T(8,128)(2,1)S(1)} %all_to_all.45) | copy-start | bytes 2359300
  87.1 48.7 %all-to-all-start.1 = ((bf16[32,32,384]{2,1,0:T(8,128)(2,1)}), bf16[32,32,384]{2,1,0:T(8,128)(2,1)S(1)}, u32[]{:S(2)}, u32[]{:S(2)}) async-start(bf16[32,32,384]{2,1,0:T(8,128)(2,1)} %bitcast.8), calls=%async_computation.1 | async-start | bytes 1572864 | tf_op jit(solution)/shard_map/all_to_all | solution.py:67
  91.2 174.7 %all-reduce.3.cloned.1.call-start = ((), (), s32[]{:S(2)}) async-start(), calls=%async_computation.5 | async-start | bytes 8388608 | tf_op jit(solution)/shard_map/psum | solution.py:75
  93.8 46.1 %copy-start.9 = (bf16[384,4]{0,1:T(4,128)(2,1)S(1)}, bf16[384,4]{0,1:T(4,128)(2,1)}, u32[]{:S(2)}) copy-start(bf16[384,4]{0,1:T(4,128)(2,1)} %param.13) | copy-start | bytes 9220
  135.8 130.1 %copy-start.7 = (bf16[32,32,384]{2,1,0:T(8,128)(2,1)}, bf16[32,32,384]{2,1,0:T(8,128)(2,1)S(1)}, u32[]{:S(2)}) copy-start(bf16[32,32,384]{2,1,0:T(8,128)(2,1)S(1)} %all-to-all-done.1) | copy-start | bytes 2359300
  265.9 3.8 copy-start.5
  269.7 49.8 %copy-start.3 = (bf16[1024,1024]{1,0:T(8,128)(2,1)S(1)}, bf16[1024,1024]{1,0:T(8,128)(2,1)}, u32[]{:S(2)}) copy-start(bf16[1024,1024]{1,0:T(8,128)(2,1)} %get-tuple-element.6) | copy-start | bytes 6291460
  271.0 24.9 %all-to-all-start.4 = ((bf16[32,32,1]{1,2,0:T(2,128)(2,1)}), bf16[32,32,1]{1,2,0:T(2,128)(2,1)S(1)}, u32[]{:S(2)}, u32[]{:S(2)}) async-start(bf16[32,32,1]{1,2,0:T(2,128)(2,1)} %convert_element_type.131), calls=%async_computation.4 | async-start | bytes 32768 | tf_op jit(solution)/shard_map/all_to_all | solution.py:91
  323.7 2.2 copy-start.4
  325.8 90.0 %all-to-all-start.3 = ((bf16[32,32,384]{2,1,0:T(8,128)(2,1)}), bf16[32,32,384]{2,1,0:T(8,128)(2,1)}, u32[]{:S(2)}, u32[]{:S(2)}) async-start(bf16[32,32,384]{2,1,0:T(8,128)(2,1)} %bitcast.50), calls=%async_computation.3 | async-start | bytes 1572864 | tf_op jit(solution)/shard_map/all_to_all | solution.py:90
  407.9 3.8 copy-start.8
Sparse Core Ops, SparseCore 0:
  140.0 125.8 all-reduce.2
where the time goes:
time: 426 us
  blocking collectives  188 us (44%)
  waiting for transfers between devices  145 us (34%)
  local copies, waits for them, and re-layouts  25.7 us (6%)
  starting transfers between devices  22.4 us (5%)
  matrix products  17.8 us (4%)
  between operations  14.9 us (3%)
  other arithmetic  12 us (3%)
    psum x1, waiting for transfers between devices, local(): lax.psum(back_part.astype(jnp.bfloat16), 'dp').astype(jnp.float32)  91.7 us
    psum x1, blocking collectives, local(): grad_router = lax.psum(router_term, 'expert')  76.7 us
    all_to_all x1, blocking collectives, local(): lax.all_to_all(send_rows, 'expert', split_axis=0, concat_axis=0, tiled=True)  61.2 us
    all_to_all x1, waiting for transfers between devices, local(): lax.all_to_all(send_grad, 'expert', split_axis=0, concat_axis=0, tiled=True)  42 us
    psum x1, blocking collectives, local(): logits = lax.psum(partial_logits, 'dp')  34.2 us
    all_to_all x1, blocking collectives, local(): lax.all_to_all(send_gate, 'expert', split_axis=0, concat_axis=0, tiled=True)  15.4 us
    all_to_all x1, starting transfers between devices, local(): lax.all_to_all(gate_part.astype(jnp.bfloat16), 'expert', split_axis=0, co...  13.2 us
    all_to_all x1, waiting for transfers between devices, local(): lax.all_to_all(gate_part.astype(jnp.bfloat16), 'expert', split_axis=0, co...  11.6 us
  transfers between devices with their start and end apart: 4, of which 3 were waited for; matrix products, arithmetic and copies ran while one was open for 3% of the time, Pallas kernels for 0%

commit v1 on v0

--- a/solution.py
+++ b/solution.py
@@ -2,9 +2,14 @@
 import jax.numpy as jnp
 from jax import lax
 from jax.sharding import PartitionSpec as P
+from jax.lax import all_gather
 
 ROOT_HALF = 0.7071067811865476
 INV_ROOT_TWO_PI = 0.3989422804014327
+
+
+def step_on_the_classes(u_in, shard_axis):
+    return jnp.sum(all_gather(u_in, axis_name=shard_axis), axis=0)
 
 
 def gelu_value(value):
@@ -72,7 +77,7 @@
     gate_column = gate_in.astype(jnp.float32)[:, None]
     before_act, back_act = (
         lax.psum(before_part.astype(jnp.bfloat16), "dp").astype(jnp.float32),
-        lax.psum(back_part.astype(jnp.bfloat16), "dp").astype(jnp.float32),
+        step_on_the_classes(back_part.astype(jnp.bfloat16), "dp").astype(jnp.float32),
     )
     gate_part, inner_grad, weighted = activate(before_act, back_act, gate_column)
     contract_rows = (((0,), (0,)), ((), ()))

time: 426 us -> 605 us (1.42)
  waiting for transfers between devices: 145 us -> 308 us
  other arithmetic: 12 us -> 28 us
    all_gather x0 -> x1, waiting for transfers between devices: none -> 212 us  [step_on_the_classes(): return jnp.sum(all_gather(u_in, axis_name=shard_axis), axis=0)]
    psum x1, waiting for transfers between devices: 91.7 us -> 42.7 us  [local(): lax.psum(before_part.astype(jnp.bfloat16), 'dp').astype(jnp.float32)]
    reduce_sum x0 -> x1, other arithmetic: none -> 13 us  [step_on_the_classes(): return jnp.sum(all_gather(u_in, axis_name=shard_axis), axis=0)]
  transfers between devices with their start and end apart: 4 -> 5, of which waited for: 3 -> 4; matrix products, arithmetic and copies ran while one was open for 3% -> 3% of each run, Pallas kernels for 0% -> 0%
where the time goes in v1:
time: 605 us; the launch traced here: 604 us
  waiting for transfers between devices  308 us (51%)
  blocking collectives  187 us (31%)
  other arithmetic  28 us (5%)
  local copies, waits for them, and re-layouts  25.7 us (4%)
  starting transfers between devices  22.3 us (4%)
  matrix products  17.8 us (3%)
  between operations  14.9 us (2%)
    all_gather x1, waiting for transfers between devices, step_on_the_classes(): return jnp.sum(all_gather(u_in, axis_name=shard_axis), axis=0)  212 us
    psum x1, blocking collectives, local(): grad_router = lax.psum(router_term, 'expert')  76.7 us
    all_to_all x1, blocking collectives, local(): lax.all_to_all(send_rows, 'expert', split_axis=0, concat_axis=0, tiled=True)  61.2 us
    psum x1, waiting for transfers between devices, local(): lax.psum(before_part.astype(jnp.bfloat16), 'dp').astype(jnp.float32)  42.7 us
    all_to_all x1, waiting for transfers between devices, local(): lax.all_to_all(send_grad, 'expert', split_axis=0, concat_axis=0, tiled=True)  41.9 us
    psum x1, blocking collectives, local(): logits = lax.psum(partial_logits, 'dp')  33.4 us
    all_to_all x1, blocking collectives, local(): lax.all_to_all(send_gate, 'expert', split_axis=0, concat_axis=0, tiled=True)  15.4 us
    reduce_sum x1, other arithmetic, step_on_the_classes(): return jnp.sum(all_gather(u_in, axis_name=shard_axis), axis=0)  13 us
  transfers between devices with their start and end apart: 5, of which 4 were waited for; matrix products, arithmetic and copies ran while one was open for 3% of the time, Pallas kernels for 0%

profile of v1, /device:TPU:1, one launch (start us, length us, event | category | flops | bytes accessed | tf_op | source)
XLA Modules:
  0.0 603.9 jit_solution(4947627519335721398)
XLA Ops:
  7.2 0.0 copy-start
  7.2 0.0 copy-start.1
  7.2 0.8 slice_bitcast_fusion.1
  8.6 0.1 pad_add_fusion
  8.7 0.1 fusion.17
  8.8 0.2 reduce_window_sum.11
  9.0 0.2 select_reduce_fusion
  9.2 0.1 fusion.52
  9.3 1.0 scatter_custom_fusion
  10.3 6.6 %gather_fusion = s32[1024]{0:T(1024)S(1)} fusion(s32[128]{0:T(128)S(1)} %scatter_custom_fusion, s32[1024]{0:T(1024)S(1)} %broadcast_clamp_fusion.2), kind=kCustom, calls=%fused_computation.2 | custom fusion | bytes 12288 | tf_op jit(solution)/shard_map/jit(_take)/gather | solution.py:65
  16.8 0.0 copy-start.2
  16.9 0.0 copy-done.1
  16.9 3.9 gather_fusion.5
  20.8 0.0 copy-done.2
  20.8 3.9 gather_fusion.4
  24.8 1.2 broadcast_select_fusion
  25.9 61.2 %all_to_all.45 = bf16[32,32,384]{2,1,0:T(8,128)(2,1)S(1)} all-to-all(bf16[32,32,384]{2,1,0:T(8,128)(2,1)S(1)} %bitcast.51), channel_id=1, replica_groups=mesh['dp'=16,'expert'=32] {'expert'}, dimensions={0} | all-to-all | bytes 1572864 | tf_op jit(solution)/shard_map/all_to_all | solution.py:71
  87.1 4.1 all-to-all-start.1
  91.2 0.0 all-reduce.2.cloned.1.call-start
  91.2 0.0 copy-done
  91.3 2.6 convolution_convert_fusion
  93.8 0.0 all-reduce.2.cloned.1.call-update
  93.8 0.0 all-gather.3.cloned.1.call-start
  93.9 41.9 %all-to-all-done.1 = bf16[32,32,384]{2,1,0:T(8,128)(2,1)S(1)} async-done(((bf16[32,32,384]{2,1,0:T(8,128)(2,1)}), bf16[32,32,384]{2,1,0:T(8,128)(2,1)S(1)}, u32[]{:S(2)}, u32[]{:S(2)}) %all-to-all-start.1) | async-done | bytes 786464 | tf_op jit(solution)/shard_map/all_to_all | solution.py:72
  135.8 4.0 convolution_convert_fusion.1
  139.8 0.0 copy-done.5
  139.8 0.0 all-gather.3.cloned.1.call-update
  139.8 0.0 copy-done.8
  139.8 0.1 fusion.58
  140.0 33.4 %psum.21 = f32[64,4]{0,1:T(4,128)S(1)} all-reduce(f32[64,4]{0,1:T(4,128)S(1)} %fusion.58), channel_id=1, replica_groups=mesh['dp'=16,'expert'=32] {'dp'}, use_global_device_ids=true, to_apply=%region_3.4 | all-reduce | flops 256 | bytes 2048 | tf_op jit(solution)/shard_map/psum | solution.py:43
  173.5 42.7 %all-reduce.2.cloned.1.call-done = bf16[1024,1024]{1,0:T(8,128)(2,1)} async-done(((bf16[1024,1024]{1,0:T(8,128)(2,1)}), bf16[1024,1024]{1,0:T(8,128)(2,1)}) %all-reduce.2.cloned.1.call-update) | async-done | bytes 2097168 | tf_op jit(solution)/shard_map/psum | solution.py:79
  216.2 4.4 fusion.9
  220.5 0.0 copy-done.6
  220.5 212.1 %all-gather.3.cloned.1.call-done = bf16[16384,1024]{1,0:T(8,128)(2,1)} async-done(((bf16[1024,1024]{1,0:T(8,128)(2,1)}), bf16[16384,1024]{1,0:T(8,128)(2,1)}) %all-gather.3.cloned.1.call-update) | async-done | bytes 33554448 | tf_op jit(solution)/shard_map/all_gather | solution.py:12
  432.6 13.0 %reduce_sum.59 = bf16[1024,1024]{1,0:T(8,128)(2,1)} reduce(bf16[16,1024,1024]{2,1,0:T(8,128)(2,1)} %bitcast.45, bf16[]{:T(256)} %constant.167.clone.1), dimensions={0}, to_apply=%region_5.7 | reduce | flops 15728640 | bytes 35651584 | tf_op jit(solution)/shard_map/reduce_sum | solution.py:12
  445.7 3.0 fusion.2
  448.7 0.7 convert_element_type.133
  449.4 13.0 %all-to-all-start.4 = ((bf16[32,32,1]{1,2,0:T(2,128)(2,1)}), bf16[32,32,1]{1,2,0:T(2,128)(2,1)S(1)}, u32[]{:S(2)}, u32[]{:S(2)}) async-start(bf16[32,32,1]{1,2,0:T(2,128)(2,1)} %convert_element_type.133), calls=%async_computation.4 | async-start | bytes 32768 | tf_op jit(solution)/shard_map/all_to_all | solution.py:96
  462.4 0.1 gather.26
  462.5 11.6 %all-to-all-done.4 = bf16[32,32,1]{1,2,0:T(2,128)(2,1)S(1)} async-done(((bf16[32,32,1]{1,2,0:T(2,128)(2,1)}), bf16[32,32,1]{1,2,0:T(2,128)(2,1)S(1)}, u32[]{:S(2)}, u32[]{:S(2)}) %all-to-all-start.4) | async-done | bytes 2080 | tf_op jit(solution)/shard_map/all_to_all | solution.py:96
  474.1 0.1 reshape.485
  474.2 1.2 gather_fusion.3
  475.4 0.1 multiply_convert_fusion.4
  475.5 6.5 %gather_fusion.1 = bf16[1024]{0:T(1024)(128)(2,1)S(1)} fusion(bf16[128]{0:T(256)(128)(2,1)S(1)} %get-tuple-element.7, s32[1024]{0:T(1024)S(1)} %broadcast_clamp_fusion.1), kind=kCustom, calls=%fused_computation.3 | custom fusion | bytes 8192 | tf_op jit(solution)/shard_map/jit(_take)/gather | solution.py:69
  482.0 0.1 gather.29
  482.2 15.4 %all_to_all.46 = bf16[32,32,1]{1,2,0:T(2,128)(2,1)S(1)} all-to-all(bf16[32,32,1]{1,2,0:T(2,128)(2,1)S(1)} %copy.11), channel_id=1, replica_groups=mesh['dp'=16,'expert'=32] {'expert'}, dimensions={0} | all-to-all | bytes 4096 | tf_op jit(solution)/shard_map/all_to_all | solution.py:73
  497.6 0.1 convert_reduce_fusion.2
  497.6 0.1 reshape.486
  497.7 0.0 copy-done.3
  497.7 4.1 fusion.1
  501.8 0.0 copy-start.4
  501.8 2.2 convolution_convert_fusion.3
  504.0 0.0 copy-done.4
  504.0 5.1 all-to-all-start.3
  509.1 0.1 slice_subtract_fusion
  509.2 0.1 convolution_bitcast_fusion
  509.3 76.7 %psum.23 = f32[384,4]{0,1:T(4,128)} all-reduce(f32[384,4]{0,1:T(4,128)S(1)} %convolution_bitcast_fusion), channel_id=1, replica_groups=mesh['dp'=16,'expert'=32] {'expert'}, use_global_device_ids=true, to_apply=%region_10.12 | all-reduce | flops 1536 | bytes 12288 | tf_op jit(solution)/shard_map/psum | solution.py:121
  586.1 3.8 convolution_convert_fusion.2
  589.9 4.2 fusion.13
  594.0 0.0 all-to-all-done.3
  594.0 1.3 convert_reduce_fusion
  595.3 0.8 gather_fusion.2
  596.1 0.1 broadcast_select_fusion.2
  596.2 0.9 fusion.14
  (21 shorter events, 0.2 us)
Async XLA Ops:
  7.2 84.1 %copy-start = (bf16[384,1024]{1,0:T(8,128)(2,1)S(1)}, bf16[384,1024]{1,0:T(8,128)(2,1)}, u32[]{:S(2)}) copy-start(bf16[384,1024]{1,0:T(8,128)(2,1)} %param.14) | copy-start | bytes 2359300
  7.2 9.7 %copy-start.1 = (bf16[64,384]{1,0:T(8,128)(2,1)S(1)}, bf16[64,384]{1,0:T(8,128)(2,1)}, u32[]{:S(2)}) copy-start(bf16[64,384]{1,0:T(8,128)(2,1)} %param.9) | copy-start | bytes 147460
  16.8 4.0 copy-start.2
  87.1 52.7 %copy-start.5 = (bf16[32,32,384]{2,1,0:T(8,128)(2,1)}, bf16[32,32,384]{2,1,0:T(8,128)(2,1)S(1)}, u32[]{:S(2)}) copy-start(bf16[32,32,384]{2,1,0:T(8,128)(2,1)S(1)} %all_to_all.45) | copy-start | bytes 2359300
  87.1 48.7 %all-to-all-start.1 = ((bf16[32,32,384]{2,1,0:T(8,128)(2,1)}), bf16[32,32,384]{2,1,0:T(8,128)(2,1)S(1)}, u32[]{:S(2)}, u32[]{:S(2)}) async-start(bf16[32,32,384]{2,1,0:T(8,128)(2,1)} %bitcast.8), calls=%async_computation.1 | async-start | bytes 1572864 | tf_op jit(solution)/shard_map/all_to_all | solution.py:72
  91.2 125.0 %all-reduce.2.cloned.1.call-start = ((), (), s32[]{:S(2)}) async-start(), calls=%async_computation.5 | async-start | bytes 4194304 | tf_op jit(solution)/shard_map/psum | solution.py:79
  93.8 46.0 %copy-start.8 = (bf16[384,4]{0,1:T(4,128)(2,1)S(1)}, bf16[384,4]{0,1:T(4,128)(2,1)}, u32[]{:S(2)}) copy-start(bf16[384,4]{0,1:T(4,128)(2,1)} %param.13) | copy-start | bytes 9220
  93.8 338.8 %all-gather.3.cloned.1.call-start = ((), (), s32[]{:S(2)}) async-start(), calls=%async_computation.6 | async-start | bytes 35651584 | tf_op jit(solution)/shard_map/all_gather | solution.py:12
  135.8 84.7 %copy-start.6 = (bf16[32,32,384]{2,1,0:T(8,128)(2,1)}, bf16[32,32,384]{2,1,0:T(8,128)(2,1)S(1)}, u32[]{:S(2)}) copy-start(bf16[32,32,384]{2,1,0:T(8,128)(2,1)S(1)} %all-to-all-done.1) | copy-start | bytes 2359300
  445.7 52.0 %copy-start.3 = (bf16[1024,1024]{1,0:T(8,128)(2,1)S(1)}, bf16[1024,1024]{1,0:T(8,128)(2,1)}, u32[]{:S(2)}) copy-start(bf16[1024,1024]{1,0:T(8,128)(2,1)} %all-reduce.2.cloned.1.call-done) | copy-start | bytes 6291460
  449.4 24.7 %all-to-all-start.4 = ((bf16[32,32,1]{1,2,0:T(2,128)(2,1)}), bf16[32,32,1]{1,2,0:T(2,128)(2,1)S(1)}, u32[]{:S(2)}, u32[]{:S(2)}) async-start(bf16[32,32,1]{1,2,0:T(2,128)(2,1)} %convert_element_type.133), calls=%async_computation.4 | async-start | bytes 32768 | tf_op jit(solution)/shard_map/all_to_all | solution.py:96
  501.8 2.2 copy-start.4
  504.0 90.0 %all-to-all-start.3 = ((bf16[32,32,384]{2,1,0:T(8,128)(2,1)}), bf16[32,32,384]{2,1,0:T(8,128)(2,1)}, u32[]{:S(2)}, u32[]{:S(2)}) async-start(bf16[32,32,384]{2,1,0:T(8,128)(2,1)} %bitcast.52), calls=%async_computation.3 | async-start | bytes 1572864 | tf_op jit(solution)/shard_map/all_to_all | solution.py:95
  586.1 3.8 copy-start.7
Sparse Core Ops, SparseCore 0:
  95.3 120.7 all-reduce.1
  219.6 212.9 all-gather.2
